TPU v7x, 256 devices: a whole 4x4x8 slice. The times are simulated.
256 devices in a mesh: dp: 16 (over z_lo, x, core), node: 16 (over z_hi, y).
Axes of the slice: x: 4, y: 4, z: 8 (z_hi: 4, z_lo: 2; z = z_hi * 2 + z_lo), core: 2. Of those that a mesh axis runs over, the one named last changes fastest.
Arguments:
- tokens: bfloat16 [131072, 3584], P(('dp', 'node')), may hold values from -6 to 6
- slot_tokens: int32 [65536], P(('dp', 'node')), may hold values from 0 to 511, as said below
- slot_counts: int32 [256], P(('dp', 'node')), may hold values from 64 to 256, as said below
- route_weight: float32 [65536], P(('dp', 'node')), may hold values from 0.25 to 1.5
- cotangent: bfloat16 [65536, 1024], P(('dp', 'node')), may hold values from -6 to 6
- weights: bfloat16 [2, 1024, 3584], P(None, 'node'), may hold values from -0.09375 to 0.09375
Outputs:
- activation: bfloat16 [65536, 1024], P(('dp', 'node'))
- token_grad: bfloat16 [131072, 3584], P(('dp', 'node'))
- weight_grad: float32 [2, 1024, 3584], P(None, 'node')
Inputs may be any that keep to these rules, and one draw needn't show every extreme that they name: `slot_tokens`: within each device's block of 256 slots the entries are distinct token indices of that device. `slot_counts`: some device uses all 256 of its slots in every draw.
All inputs are finite; a program needn't handle non-finite values.
Results may differ from a plain program's by a relative error of at most 0.015.
Values may be sent and summed in bfloat16 or wider, within the bound.
No kernel may reach another device: no remote copies, remote signals or barrier semaphores. Data moves between devices by JAX's collectives and lax.ppermute only.
A program may use at most 128 MiB of HBM per device.

v0:
```python
import jax
import jax.numpy as jnp
from jax import lax
from jax.sharding import PartitionSpec as P


def local(tokens, slot_tokens, slot_counts, route_weight, cotangent, weights):
    slots = slot_tokens.shape[0]
    total_slots = slots * lax.axis_size("dp") * lax.axis_size("node")
    factor = 1.0 / total_slots**0.5
    picked = tokens[slot_tokens]
    gathered = lax.all_gather(weights, "node", axis=1, tiled=True)
    pre = jnp.einsum("kd,chd->ckh", picked, gathered, preferred_element_type=jnp.float32)
    gate = pre[0]
    upval = pre[1]
    used = (jnp.arange(slots, dtype=jnp.int32) < slot_counts[0]).astype(jnp.float32)[:, None]
    scale = route_weight[:, None]
    sigma = jax.nn.sigmoid(gate)
    activation = (used * scale * gate * sigma * upval).astype(jnp.bfloat16)
    scaled = cotangent.astype(jnp.float32) * scale * used
    up_grad = (scaled * gate * sigma).astype(jnp.bfloat16)
    gate_grad = (scaled * upval * sigma * (1.0 + gate * (1.0 - sigma))).astype(jnp.bfloat16)
    stacked = jnp.stack([gate_grad, up_grad])
    slot_grad = jnp.einsum("ckh,chd->kd", stacked, gathered, preferred_element_type=jnp.float32)
    token_grad = (
        jnp.zeros(tokens.shape, jnp.float32).at[slot_tokens].add(slot_grad).astype(jnp.bfloat16)
    )
    partial_term = (
        jnp.einsum("kd,ckh->chd", picked, stacked, preferred_element_type=jnp.float32) * factor
    ).astype(jnp.bfloat16)
    partial_term = lax.optimization_barrier(partial_term).astype(jnp.float32)
    panel_sum = lax.psum_scatter(
        partial_term.astype(jnp.bfloat16), "node", scatter_dimension=1, tiled=True
    ).astype(jnp.float32)
    weight_grad = lax.psum(panel_sum, "dp")
    return (activation, token_grad, weight_grad)


def solution(mesh):
    placed = (
        P(("dp", "node"), None),
        P(("dp", "node")),
        P(("dp", "node")),
        P(("dp", "node")),
        P(("dp", "node"), None),
        P(None, "node", None),
    )
    return jax.shard_map(
        local,
        mesh=mesh,
        in_specs=placed,
        out_specs=(P(("dp", "node"), None), P(("dp", "node"), None), P(None, "node", None)),
        check_vma=False,
    )
```

profile of v0, /device:TPU:40, one launch (start us, length us, event | category | flops | bytes accessed | tf_op | source)
XLA Modules:
  0.0 468.8 jit_solution(10295132528529006540)
XLA Ops:
  7.2 0.0 all-gather.2.cloned.1.call-start
  7.2 0.7 all-gather.2.cloned.1.call-update
  7.9 0.0 reduce-scatter.2.cloned.1.call-start
  8.6 0.7 compare_select_fusion
  9.3 0.0 copy-start.1
  9.3 6.1 %gather_fusion = bf16[256,3584]{1,0:T(8,128)(2,1)S(1)} fusion(bf16[512,3584]{1,0:T(8,128)(2,1)} %param.6, s32[1024]{0:T(1024)S(1)} %pad_clamp_fusion), kind=kCustom, calls=%fused_computation | custom fusion | bytes 3671040 | tf_op jit(solution)/shard_map/gather | solution.py:11
  15.4 0.0 copy-done.1
  15.4 0.0 copy-start
  15.4 177.5 %all-gather.2.cloned.1.call-done = bf16[2,1024,3584]{2,1,0:T(8,128)(2,1)} async-done(((bf16[2,64,3584]{2,1,0:T(8,128)(2,1)}), bf16[2,1024,3584]{2,1,0:T(8,128)(2,1)}) %all-gather.2.cloned.1.call-update) | async-done | bytes 14680080 | tf_op jit(solution)/shard_map/all_gather | solution.py:12
  192.9 7.3 %fusion.5 = f32[2,256,1024]{2,1,0:T(8,128)S(1)} fusion(bf16[2,1024,3584]{2,1,0:T(8,128)(2,1)} %all-gather.2.cloned.1.call-done, bf16[256,3584]{1,0:T(8,128)(2,1)S(1)} %gather_fusion), kind=kOutput, calls=%fused_computation.9 | convolution fusion | flops 3758096384 | bytes 18612224 | tf_op jit(solution)/shard_map/kd,chd->ckh/dot_general | solution.py:13
  200.2 0.0 copy-done
  200.2 1.6 fusion.9
  201.8 7.4 %multiply_convert_fusion = bf16[2,1024,3584]{2,1,0:T(8,128)(2,1)} fusion(bf16[256,3584]{1,0:T(8,128)(2,1)S(1)} %gather_fusion, bf16[1,256,1024]{2,1,0:T(8,128)(2,1)S(1)} %get-tuple-element.4, bf16[1,256,1024]{2,1,0:T(8,128)(2,1)S(1)} %get-tuple-element.3), kind=kOutput, calls=%fused_computation.2 | convolution fusion | flops 3773300736 | bytes 17563648 | tf_op jit(solution)/shard_map/kd,ckh->chd/dot_general | solution.py:29
  209.2 0.0 reduce-scatter.2.cloned.1.call-update
  209.2 9.1 %convolution_bitcast_fusion = f32[256,3584]{1,0:T(8,128)} fusion(bf16[2,1024,3584]{2,1,0:T(8,128)(2,1)} %all-gather.2.cloned.1.call-done, bf16[1,256,1024]{2,1,0:T(8,128)(2,1)S(1)} %get-tuple-element.4, bf16[1,256,1024]{2,1,0:T(8,128)(2,1)S(1)} %get-tuple-element.3), kind=kOutput, calls=%fused_computation.3 | convolution fusion | flops 3758620672 | bytes 19398656 | tf_op jit(solution)/shard_map/ckh,chd->kd/dot_general | solution.py:24
  218.3 10.5 %scatter_custom_fusion = f32[512,3584]{1,0:T(8,128)} fusion(s32[256]{0:T(256)S(1)} %compare_select_fusion, f32[256,3584]{1,0:T(8,128)} %convolution_bitcast_fusion, f32[]{:T(128)} %constant.1.clone.1), kind=kCustom, calls=%fused_computation.4 | custom fusion | flops 917504 | bytes 7340544 | tf_op jit(solution)/shard_map/scatter-add | solution.py:26
  228.8 5.3 %convert_element_type.35 = bf16[512,3584]{1,0:T(8,128)(2,1)} convert(f32[512,3584]{1,0:T(8,128)} %scatter_custom_fusion) | non-fusion elementwise | flops 1835008 | bytes 11010048 | tf_op jit(solution)/shard_map/convert_element_type | solution.py:26
  234.2 157.4 %reduce-scatter.2.cloned.1.call-done = bf16[2,64,3584]{2,1,0:T(8,128)(2,1)} async-done(((bf16[2,1024,3584]{2,1,0:T(8,128)(2,1)}), bf16[2,64,3584]{2,1,0:T(8,128)(2,1)}) %reduce-scatter.2.cloned.1.call-update) | async-done | bytes 917520 | tf_op jit(solution)/shard_map/reduce_scatter | solution.py:32
  391.6 70.4 %all-reduce.1 = f32[2,64,3584]{2,1,0:T(8,128)} all-reduce(bf16[2,64,3584]{2,1,0:T(8,128)(2,1)} %reduce-scatter.2.cloned.1.call-done), channel_id=1, replica_groups=mesh['dp'=16,'node'=16] {'dp'}, use_global_device_ids=true, to_apply=%region_2.0 | all-reduce | flops 458752 | bytes 2752512 | tf_op jit(solution)/shard_map/psum | solution.py:35
  (3 shorter events, 0.0 us)
Async XLA Ops:
  7.2 185.7 %all-gather.2.cloned.1.call-start = ((), (), s32[]{:S(2)}) async-start(), calls=%async_computation.1 | async-start | bytes 15597568 | tf_op jit(solution)/shard_map/all_gather | solution.py:12
  7.9 383.7 %reduce-scatter.2.cloned.1.call-start = ((), (), s32[]{:S(2)}) async-start(), calls=%async_computation.2 | async-start | bytes 15597568 | tf_op jit(solution)/shard_map/reduce_scatter | solution.py:32
  9.3 6.1 %copy-start.1 = (f32[256]{0:T(256)S(1)}, f32[256]{0:T(256)}, u32[]{:S(2)}) copy-start(f32[256]{0:T(256)} %param.9) | copy-start | bytes 3076
  15.4 184.8 %copy-start = (bf16[256,1024]{1,0:T(8,128)(2,1)S(1)}, bf16[256,1024]{1,0:T(8,128)(2,1)}, u32[]{:S(2)}) copy-start(bf16[256,1024]{1,0:T(8,128)(2,1)} %param.10) | copy-start | bytes 1572868
Sparse Core Ops, SparseCore 0:
  10.4 182.4 all-gather.1
  209.3 182.2 reduce-scatter.1
where the time goes:
time: 469 us
  waiting for transfers between devices  336 us (72%)
  blocking collectives  70.4 us (15%)
  matrix products  23.8 us (5%)
  other arithmetic  18.1 us (4%)
  between operations  14.7 us (3%)
  local copies, waits for them, and re-layouts  6.06 us (1%)
    all_gather x1, waiting for transfers between devices, local(): gathered = lax.all_gather(weights, 'node', axis=1, tiled=True)  178 us
    reduce_scatter x1, waiting for transfers between devices, local(): lax.psum_scatter(partial_term.astype(jnp.bfloat16), 'node', scatter_dimen...  157 us
    psum x1, blocking collectives, local(): weight_grad = lax.psum(panel_sum, 'dp')  70.4 us
    scatter-add x1, other arithmetic, local(): jnp.zeros(tokens.shape, jnp.float32).at[slot_tokens].add(slot_grad)  10.5 us
  transfers between devices with their start and end apart: 2, of which 2 were waited for; matrix products, arithmetic and copies ran while one was open for 7% of the time, Pallas kernels for 0%

commit v1 on v0

--- a/solution.py
+++ b/solution.py
@@ -9,7 +9,9 @@
     total_slots = slots * lax.axis_size("dp") * lax.axis_size("node")
     factor = 1.0 / total_slots**0.5
     picked = tokens[slot_tokens]
-    gathered = lax.all_gather(weights, "node", axis=1, tiled=True)
+    gathered = jnp.concatenate(
+        lax.all_to_all(jnp.stack([weights] * lax.axis_size("node")), "node", 0, 0), axis=1
+    )
     pre = jnp.einsum("kd,chd->ckh", picked, gathered, preferred_element_type=jnp.float32)
     gate = pre[0]
     upval = pre[1]

time: 469 us -> 638 us (1.36)
  waiting for transfers between devices: 336 us -> 475 us
  local copies, waits for them, and re-layouts: 6.06 us -> 27.6 us
  starting transfers between devices: 0.08 us -> 10.8 us
    all_to_all x0 -> x1, waiting for transfers between devices: none -> 315 us  [local(): lax.all_to_all(jnp.stack([weights] * lax.axis_size('node')), 'node', 0, 0)]
    all_gather x1 -> x0, waiting for transfers between devices: 178 us -> none  [local(): gathered = lax.all_gather(weights, 'node', axis=1, tiled=True)]
    reshape x0 -> x1, local copies, waits for them, and re-layouts: none -> 13.5 us  [local(): jnp.concatenate(lax.all_to_all(jnp.stack([weights] * lax.axis_size('node'...]
    all_to_all x0 -> x1, starting transfers between devices: none -> 10.8 us  [local(): lax.all_to_all(jnp.stack([weights] * lax.axis_size('node')), 'node', 0, 0)]
    another operation x0 -> x1, local copies, waits for them, and re-layouts: none -> 8.02 us  [local(): jnp.stack([weights] * lax.axis_size('node'))]
  transfers between devices with their start and end apart: 2 -> 2, of which waited for: 2 -> 2; matrix products, arithmetic and copies ran while one was open for 7% -> 5% of each run, Pallas kernels for 0% -> 0%
where the time goes in v1:
time: 638 us; the launch traced here: 637 us
  waiting for transfers between devices  475 us (74%)
  blocking collectives  67.9 us (11%)
  local copies, waits for them, and re-layouts  27.6 us (4%)
  matrix products  23.8 us (4%)
  other arithmetic  17.1 us (3%)
  between operations  14.8 us (2%)
  starting transfers between devices  10.8 us (2%)
    all_to_all x1, waiting for transfers between devices, local(): lax.all_to_all(jnp.stack([weights] * lax.axis_size('node')), 'node', 0, 0)  315 us
    reduce_scatter x1, waiting for transfers between devices, local(): lax.psum_scatter(partial_term.astype(jnp.bfloat16), 'node', scatter_dimen...  160 us
    psum x1, blocking collectives, local(): weight_grad = lax.psum(panel_sum, 'dp')  67.9 us
    reshape x1, local copies, waits for them, and re-layouts, local(): jnp.concatenate(lax.all_to_all(jnp.stack([weights] * lax.axis_size('node'...  13.5 us
  transfers between devices with their start and end apart: 2, of which 2 were waited for; matrix products, arithmetic and copies ran while one was open for 5% of the time, Pallas kernels for 0%

profile of v1, /device:TPU:40, one launch (start us, length us, event | category | flops | bytes accessed | tf_op | source)
XLA Modules:
  0.0 636.9 jit_solution(2191060021564918289)
XLA Ops:
  7.2 8.0 %stack.8 = bf16[16,2,64,3584]{3,2,1,0:T(8,128)(2,1)} broadcast(bf16[2,64,3584]{2,1,0:T(8,128)(2,1)} %param.11), dimensions={1,2,3} | broadcast | bytes 15597568 | tf_op jit(solution)/shard_map/stack | solution.py:13
  15.2 0.0 copy-start.2
  15.2 10.8 %all-to-all-start = ((bf16[16,2,64,3584]{3,2,1,0:T(8,128)(2,1)}), bf16[16,2,64,3584]{3,2,1,0:T(8,128)(2,1)}, u32[]{:S(2)}, u32[]{:S(2)}) async-start(bf16[16,2,64,3584]{3,2,1,0:T(8,128)(2,1)} %stack.8), calls=%async_computation | async-start | bytes 29360128 | tf_op jit(solution)/shard_map/all_to_all | solution.py:13
  26.0 0.0 reduce-scatter.2.cloned.1.call-start
  26.7 0.0 copy-done.2
  26.7 0.0 copy-start.1
  26.7 6.0 gather_fusion
  32.8 0.0 copy-done.1
  32.8 314.6 %all-to-all-done = bf16[16,2,64,3584]{3,2,1,0:T(8,128)(2,1)} async-done(((bf16[16,2,64,3584]{3,2,1,0:T(8,128)(2,1)}), bf16[16,2,64,3584]{3,2,1,0:T(8,128)(2,1)}, u32[]{:S(2)}, u32[]{:S(2)}) %all-to-all-start) | async-done | bytes 14680096 | tf_op jit(solution)/shard_map/all_to_all | solution.py:13
  347.4 13.5 %copy.11 = bf16[2,16,64,3584]{3,2,1,0:T(8,128)(2,1)} copy(bf16[2,16,64,3584]{3,2,0,1:T(8,128)(2,1)} %bitcast.2) | data formatting | bytes 29360128 | tf_op jit(solution)/shard_map/reshape | solution.py:12
  360.8 0.0 copy-start
  360.8 7.3 %fusion.5 = f32[2,256,1024]{2,1,0:T(8,128)S(1)} fusion(bf16[2,1024,3584]{2,1,0:T(8,128)(2,1)} %bitcast.50, bf16[256,3584]{1,0:T(8,128)(2,1)S(1)} %gather_fusion), kind=kOutput, calls=%fused_computation.9 | convolution fusion | flops 3758096384 | bytes 18612224 | tf_op jit(solution)/shard_map/kd,chd->ckh/dot_general | solution.py:15
  368.2 0.0 copy-done
  368.2 1.6 fusion.9
  369.8 7.4 %multiply_convert_fusion = bf16[2,1024,3584]{2,1,0:T(8,128)(2,1)} fusion(bf16[256,3584]{1,0:T(8,128)(2,1)S(1)} %gather_fusion, bf16[1,256,1024]{2,1,0:T(8,128)(2,1)S(1)} %get-tuple-element.4, bf16[1,256,1024]{2,1,0:T(8,128)(2,1)S(1)} %get-tuple-element.3), kind=kOutput, calls=%fused_computation.2 | convolution fusion | flops 3773300736 | bytes 17563648 | tf_op jit(solution)/shard_map/kd,ckh->chd/dot_general | solution.py:31
  377.2 0.0 reduce-scatter.2.cloned.1.call-update
  377.2 9.1 %convolution_bitcast_fusion = f32[256,3584]{1,0:T(8,128)} fusion(bf16[2,1024,3584]{2,1,0:T(8,128)(2,1)} %bitcast.51, bf16[1,256,1024]{2,1,0:T(8,128)(2,1)S(1)} %get-tuple-element.4, bf16[1,256,1024]{2,1,0:T(8,128)(2,1)S(1)} %get-tuple-element.3), kind=kOutput, calls=%fused_computation.3 | convolution fusion | flops 3758620672 | bytes 19398656 | tf_op jit(solution)/shard_map/ckh,chd->kd/dot_general | solution.py:26
  386.3 10.2 %scatter_custom_fusion = f32[512,3584]{1,0:T(8,128)} fusion(s32[256]{0:T(256)S(1)} %compare_select_fusion, f32[256,3584]{1,0:T(8,128)} %convolution_bitcast_fusion, f32[]{:T(128)} %constant.1.clone.1), kind=kCustom, calls=%fused_computation.4 | custom fusion | flops 917504 | bytes 7340544 | tf_op jit(solution)/shard_map/scatter-add | solution.py:28
  396.4 5.3 convert_element_type.35
  401.8 160.4 %reduce-scatter.2.cloned.1.call-done = bf16[2,64,3584]{2,1,0:T(8,128)(2,1)} async-done(((bf16[2,1024,3584]{2,1,0:T(8,128)(2,1)}), bf16[2,64,3584]{2,1,0:T(8,128)(2,1)}) %reduce-scatter.2.cloned.1.call-update) | async-done | bytes 917520 | tf_op jit(solution)/shard_map/reduce_scatter | solution.py:34
  562.2 67.9 %all-reduce.1 = f32[2,64,3584]{2,1,0:T(8,128)} all-reduce(bf16[2,64,3584]{2,1,0:T(8,128)(2,1)} %reduce-scatter.2.cloned.1.call-done), channel_id=1, replica_groups=mesh['dp'=16,'node'=16] {'dp'}, use_global_device_ids=true, to_apply=%region_2.0 | all-reduce | flops 458752 | bytes 2752512 | tf_op jit(solution)/shard_map/psum | solution.py:37
  (4 shorter events, 0.0 us)
Async XLA Ops:
  15.2 11.5 %copy-start.2 = (s32[256]{0:T(256)S(1)}, s32[256]{0:T(256)}, u32[]{:S(2)}) copy-start(s32[256]{0:T(256)} %param.7) | copy-start | bytes 3076
  15.2 332.2 %all-to-all-start = ((bf16[16,2,64,3584]{3,2,1,0:T(8,128)(2,1)}), bf16[16,2,64,3584]{3,2,1,0:T(8,128)(2,1)}, u32[]{:S(2)}, u32[]{:S(2)}) async-start(bf16[16,2,64,3584]{3,2,1,0:T(8,128)(2,1)} %stack.8), calls=%async_computation | async-start | bytes 29360128 | tf_op jit(solution)/shard_map/all_to_all | solution.py:13
  26.0 536.2 %reduce-scatter.2.cloned.1.call-start = ((), (), s32[]{:S(2)}) async-start(), calls=%async_computation.2 | async-start | bytes 15597568 | tf_op jit(solution)/shard_map/reduce_scatter | solution.py:34
  26.7 6.1 copy-start.1
  360.8 7.4 %copy-start = (bf16[256,1024]{1,0:T(8,128)(2,1)S(1)}, bf16[256,1024]{1,0:T(8,128)(2,1)}, u32[]{:S(2)}) copy-start(bf16[256,1024]{1,0:T(8,128)(2,1)} %param.10) | copy-start | bytes 1572868
Sparse Core Ops, SparseCore 0:
  377.3 184.8 reduce-scatter.1
